TPU v7x, 128 devices: a whole 4x4x4 slice. The times are simulated.
128 devices in a mesh: dp: 16 (over x_lo, y, core), fsdp: 8 (over z, x_hi).
Axes of the slice: x: 4 (x_hi: 2, x_lo: 2; x = x_hi * 2 + x_lo), y: 4, z: 4, core: 2. Of those that a mesh axis runs over, the one named last changes fastest.
Arguments:
- tokens: bfloat16 [65536, 8192], P(('dp', 'fsdp')), may hold values from -24 to 24
- out_grad: bfloat16 [65536, 1024], P(('dp', 'fsdp')), may hold values from -0.5 to 0.5
- weight_codes: bfloat16 [8192, 1024], P('fsdp'), may hold values from -127 to 127
- block_scales: float32 [8192, 8], P('fsdp'), may hold values from 0.003 to 0.03
- proj_basis: bfloat16 [1024, 512], replicated, may hold values from -0.1875 to 0.1875
- first_prev: float32 [8192, 512], P('fsdp', 'dp'), may hold values from -6 to 6
- second_prev: float32 [8192, 512], P('fsdp', 'dp'), may hold values from 0.5 to 4
Outputs:
- input_grad: bfloat16 [65536, 8192], P(('dp', 'fsdp'))
- first_new: float32 [8192, 512], P('fsdp', 'dp')
- second_new: float32 [8192, 512], P('fsdp', 'dp')
- new_weight: bfloat16 [8192, 1024], P('fsdp')
All inputs are finite; a program needn't handle non-finite values.
Results may differ from a plain program's by a relative error of at most 0.015.
Values may be sent and summed in bfloat16 or wider, within the bound.
A program may use at most 128 MiB of HBM per device.

v0:
```python
import jax
import jax.numpy as jnp
from jax import lax
from jax.sharding import PartitionSpec as P

beta_one = 0.9
beta_two = 0.999
learn_rate = 0.2
epsilon = 1e-08


def dequantize(weight_codes, block_scales):
    height = weight_codes.shape[0]
    breadth = weight_codes.shape[1]
    groups = block_scales.shape[1]
    blocks = (
        weight_codes.reshape(height, groups, breadth // groups).astype(jnp.float32)
        * block_scales[:, :, None]
    )
    return blocks.reshape(height, breadth).astype(jnp.bfloat16)


def shards(tokens, out_grad, weight_codes, block_scales, proj_basis, first_prev, second_prev):
    weight = dequantize(weight_codes, block_scales)
    input_grad = lax.dot_general(
        out_grad,
        lax.all_gather(weight, "fsdp", axis=0, tiled=True),
        (((1,), (1,)), ((), ())),
        preferred_element_type=jnp.float32,
    ).astype(jnp.bfloat16)
    projected = jnp.dot(out_grad, proj_basis, preferred_element_type=jnp.float32).astype(
        jnp.bfloat16
    )
    full_term = lax.dot_general(
        tokens, projected, (((0,), (0,)), ((), ())), preferred_element_type=jnp.float32
    )
    col_shares = lax.psum_scatter(
        full_term.astype(jnp.bfloat16), "dp", scatter_dimension=1, tiled=True
    )
    low_grad = lax.psum_scatter(col_shares, "fsdp", scatter_dimension=0, tiled=True).astype(
        jnp.float32
    )
    first_new = beta_one * first_prev + (1.0 - beta_one) * low_grad
    second_new = beta_two * second_prev + (1.0 - beta_two) * low_grad * low_grad
    step_low = (first_new / (jnp.sqrt(second_new) + epsilon)).astype(jnp.bfloat16)
    change = lax.dot_general(
        lax.all_gather(step_low, "dp", axis=1, tiled=True),
        proj_basis,
        (((1,), (1,)), ((), ())),
        preferred_element_type=jnp.float32,
    )
    new_weight = (weight.astype(jnp.float32) - learn_rate * change).astype(jnp.bfloat16)
    return (input_grad, first_new, second_new, new_weight)


def solution(mesh):
    in_specs = (
        P(("dp", "fsdp"), None),
        P(("dp", "fsdp"), None),
        P("fsdp", None),
        P("fsdp", None),
        P(),
        P("fsdp", "dp"),
        P("fsdp", "dp"),
    )
    out_specs = (P(("dp", "fsdp"), None), P("fsdp", "dp"), P("fsdp", "dp"), P("fsdp", None))
    return jax.shard_map(shards, mesh=mesh, in_specs=in_specs, out_specs=out_specs, check_vma=False)
```

profile of v0, /device:TPU:1, one launch (start us, length us, event | category | flops | bytes accessed | tf_op | source)
XLA Modules:
  0.0 424.8 jit_solution(17280535367291936860)
XLA Ops:
  7.2 0.0 copy-start
  7.2 0.0 reduce-scatter.3.cloned.1.call-start
  7.2 1.2 copy-done
  8.4 10.5 %fusion.1 = bf16[8192,512]{0,1:T(8,128)(2,1)} fusion(bf16[512,8192]{1,0:T(8,128)(2,1)} %param.7, bf16[512,1024]{1,0:T(8,128)(2,1)S(1)} %copy-done, bf16[1024,512]{1,0:T(8,128)(2,1)} %param.11), kind=kOutput, calls=%fused_computation.3 | convolution fusion | flops 4836294656 | bytes 18874368 | tf_op jit(solution)/shard_map/dot_general | solution.py:34
  18.9 0.0 copy-start.3
  18.9 0.0 copy-start.4
  18.9 0.0 copy-start.5
  18.9 0.0 reduce-scatter.3.cloned.1.call-update
  19.0 0.0 reduce-scatter.5.cloned.1.call-start
  19.0 74.1 %reduce-scatter.3.cloned.1.call-done = bf16[8192,32]{0,1:T(8,128)(2,1)} async-done(((bf16[8192,512]{0,1:T(8,128)(2,1)}), bf16[8192,32]{0,1:T(8,128)(2,1)}) %reduce-scatter.3.cloned.1.call-update) | async-done | bytes 524304 | tf_op jit(solution)/shard_map/reduce_scatter | solution.py:37
  93.1 0.0 reduce-scatter.5.cloned.1.call-update
  93.1 0.0 all-gather.5.cloned.1.call-start
  93.2 74.9 %reduce-scatter.5.cloned.1.call-done = bf16[1024,32]{0,1:T(8,128)(2,1)} async-done(((bf16[8192,32]{0,1:T(8,128)(2,1)}), bf16[1024,32]{0,1:T(8,128)(2,1)}) %reduce-scatter.5.cloned.1.call-update) | async-done | bytes 65552 | tf_op jit(solution)/shard_map/reduce_scatter | solution.py:40
  168.1 0.0 copy-done.3
  168.1 0.0 copy-done.4
  168.1 1.6 divide_convert_fusion
  169.7 0.0 all-gather.5.cloned.1.call-update
  169.7 0.0 all-gather.3.cloned.1.call-start
  169.8 0.0 copy-done.5
  169.8 0.2 copy.11
  170.0 0.0 copy-start.1
  170.0 1.1 mul.44
  171.1 0.4 copy-done.1
  171.6 0.0 copy-start.2
  171.6 2.5 fusion.2
  174.0 0.0 all-gather.3.cloned.1.call-update
  174.1 30.1 %all-gather.5.cloned.1.call-done = bf16[1024,512]{0,1:T(8,128)(2,1)} async-done(((bf16[1024,32]{0,1:T(8,128)(2,1)}), bf16[1024,512]{0,1:T(8,128)(2,1)}) %all-gather.5.cloned.1.call-update) | async-done | bytes 1048592 | tf_op jit(solution)/shard_map/all_gather | solution.py:47
  204.1 0.0 copy-done.2
  204.2 4.5 %subtract_convert_fusion = bf16[1024,1024]{1,0:T(8,128)(2,1)} fusion(bf16[1024,1024]{1,0:T(8,128)(2,1)} %fusion.2, bf16[1024,512]{0,1:T(8,128)(2,1)} %all-gather.5.cloned.1.call-done, bf16[1024,512]{1,0:T(8,128)(2,1)S(1)} %copy-done.2), kind=kOutput, calls=%fused_computation.6 | convolution fusion | flops 1077936128 | bytes 6291456 | tf_op jit(solution)/shard_map/dot_general | solution.py:46
  208.7 180.7 %all-gather.3.cloned.1.call-done = bf16[8192,1024]{1,0:T(8,128)(2,1)} async-done(((bf16[1024,1024]{1,0:T(8,128)(2,1)}), bf16[8192,1024]{1,0:T(8,128)(2,1)}) %all-gather.3.cloned.1.call-update) | async-done | bytes 16777232 | tf_op jit(solution)/shard_map/all_gather | solution.py:27
  389.4 16.9 %fusion = bf16[512,8192]{0,1:T(8,128)(2,1)} fusion(bf16[8192,1024]{1,0:T(8,128)(2,1)} %all-gather.3.cloned.1.call-done, bf16[512,1024]{1,0:T(8,128)(2,1)S(1)} %copy-done), kind=kOutput, calls=%fused_computation.2 | convolution fusion | flops 8594128896 | bytes 26214400 | tf_op jit(solution)/shard_map/dot_general | solution.py:25
  406.4 11.9 %copy.12 = bf16[512,8192]{1,0:T(8,128)(2,1)} copy(bf16[512,8192]{0,1:T(8,128)(2,1)} %fusion) | data formatting | bytes 16777216
Async XLA Ops:
  7.2 1.2 copy-start
  7.2 85.9 %reduce-scatter.3.cloned.1.call-start = ((), (), s32[]{:S(2)}) async-start(), calls=%async_computation.3 | async-start | bytes 8912896 | tf_op jit(solution)/shard_map/reduce_scatter | solution.py:37
  18.9 149.2 %copy-start.3 = (f32[1024,32]{0,1:T(8,128)S(1)}, f32[1024,32]{0,1:T(8,128)}, u32[]{:S(2)}) copy-start(f32[1024,32]{0,1:T(8,128)} %param.13) | copy-start | bytes 393220
  18.9 149.2 %copy-start.4 = (f32[1024,32]{0,1:T(8,128)S(1)}, f32[1024,32]{0,1:T(8,128)}, u32[]{:S(2)}) copy-start(f32[1024,32]{0,1:T(8,128)} %param.12) | copy-start | bytes 393220
  18.9 150.8 %copy-start.5 = (f32[1024,8]{0,1:T(8,128)S(1)}, f32[1024,8]{0,1:T(8,128)}, u32[]{:S(2)}) copy-start(f32[1024,8]{0,1:T(8,128)} %param.10) | copy-start | bytes 98308
  19.0 149.1 %reduce-scatter.5.cloned.1.call-start = ((), (), s32[]{:S(2)}) async-start(), calls=%async_computation.4 | async-start | bytes 589824 | tf_op jit(solution)/shard_map/reduce_scatter | solution.py:40
  93.1 111.0 %all-gather.5.cloned.1.call-start = ((), (), s32[]{:S(2)}) async-start(), calls=%async_computation.5 | async-start | bytes 1114112 | tf_op jit(solution)/shard_map/all_gather | solution.py:47
  169.7 219.7 %all-gather.3.cloned.1.call-start = ((), (), s32[]{:S(2)}) async-start(), calls=%async_computation.2 | async-start | bytes 18874368 | tf_op jit(solution)/shard_map/all_gather | solution.py:27
  170.0 1.6 copy-start.1
  171.6 32.6 %copy-start.2 = (bf16[1024,512]{1,0:T(8,128)(2,1)S(1)}, bf16[1024,512]{1,0:T(8,128)(2,1)}, u32[]{:S(2)}) copy-start(bf16[1024,512]{1,0:T(8,128)(2,1)} %param.11) | copy-start | bytes 3145732
Sparse Core Ops, SparseCore 0:
  19.1 73.9 reduce-scatter.2
  96.7 71.3 reduce-scatter.4
  170.5 33.6 all-gather.4
  207.2 182.1 all-gather.2
where the time goes:
time: 425 us
  waiting for transfers between devices  360 us (85%)
  matrix products  32 us (8%)
  local copies, waits for them, and re-layouts  14.9 us (4%)
  between operations  13.8 us (3%)
    all_gather x1, waiting for transfers between devices, shards(): lax.all_gather(weight, 'fsdp', axis=0, tiled=True)  181 us
    reduce_scatter x1, waiting for transfers between devices, shards(): lax.psum_scatter(col_shares, 'fsdp', scatter_dimension=0, tiled=True)  74.9 us
    reduce_scatter x1, waiting for transfers between devices, shards(): lax.psum_scatter(full_term.astype(jnp.bfloat16), 'dp', scatter_dimension=...  74.1 us
    all_gather x1, waiting for transfers between devices, shards(): lax.all_gather(step_low, 'dp', axis=1, tiled=True)  30.1 us
    dot_general x1, matrix products, shards(): lax.dot_general(out_grad, lax.all_gather(weight, 'fsdp', axis=0, tiled=Tr...  16.9 us
    unnamed x14, local copies, waits for them, and re-layouts  13.7 us
    dot_general x1, matrix products, shards(): lax.dot_general(tokens, projected, (((0,), (0,)), ((), ())), preferred_el...  10.5 us
  transfers between devices with their start and end apart: 4, of which 4 were waited for; matrix products, arithmetic and copies ran while one was open for 2% of the time, Pallas kernels for 0%

commit v1 on v0

v1 whole, which is shorter than its diff:
```python
import functools

import jax
import jax.numpy as jnp
from jax import lax
from jax.experimental import pallas as pl
from jax.experimental.pallas import tpu as pltpu
from jax.sharding import PartitionSpec as P

MESH = pl.DeviceIdType.MESH
BF16 = jnp.bfloat16
F32 = jnp.float32
beta_one = 0.9
beta_two = 0.999
learn_rate = 0.2
epsilon = 1e-08

D = 8192
N = 1024
RANK = 512
TOK = 512
LAG = 2
NT = (((1,), (1,)), ((), ()))


class Net:
    def __init__(self, send_sems, recv_sems):
        self.send_sems, self.recv_sems = send_sems, recv_sems
        self.table = {}
        self.sent, self.got = set(), set()

    def start(self, name, src, dst, device):
        at = len(self.table)
        copy = pltpu.make_async_remote_copy(
            src_ref=src,
            dst_ref=dst,
            send_sem=self.send_sems.at[at],
            recv_sem=self.recv_sems.at[at],
            device_id=device,
            device_id_type=MESH,
        )
        self.table[name] = copy
        copy.start()

    def recv(self, name):
        if name not in self.got:
            self.got.add(name)
            self.table[name].wait_recv()

    def finish(self):
        for name, copy in self.table.items():
            self.recv(name)
        for name, copy in self.table.items():
            copy.wait_send()


COPIES = 128


def exchange(
    tokens, out_grad, codes, scales, basis, first_prev, second_prev,
    ig, step_all, first_new, second_new, weight,
    W, og, stage, cod, sca, bas, tok, proj_t, sib_out, sib_in, own, cs, rr, s2, y_in, cs2, x_in, z_out, z_in,
    fp, sp, send_sems, recv_sems, load_sems,
):
    d = lax.axis_index("dp")
    f = lax.axis_index("fsdp")
    xlo, y, c = d // 8, (d // 2) % 4, d % 2
    z, xhi = f // 2, f % 2

    def dev(dx=0, dh=0, dy=0, dz=0, dc=0):
        xl = 1 - xlo if dx else xlo
        xh = 1 - xhi if dh else xhi
        cc = 1 - c if dc else c
        return (xl * 8 + ((y + dy) % 4) * 2 + cc, ((z + dz) % 4) * 2 + xh)

    sib = dev(dc=1)
    zp, zm = dev(dz=1), dev(dz=3)
    yp, ym = dev(dy=1), dev(dy=3)
    xc, xs, xo = dev(dx=1, dh=1), dev(dx=1), dev(dh=1)
    peers = [sib, zp, zm, dev(dz=2), xc, xs, xo] + [dev(dx=j // 4, dy=j % 4) for j in (1, 2, 3, 5, 6, 7)]

    loads = {}

    def load(name, src, dst):
        copy = pltpu.make_async_copy(src, dst, load_sems.at[len(loads)])
        loads[name] = copy
        copy.start()

    half = pl.multiple_of(c * 512, 512)
    other = pl.multiple_of(512 - c * 512, 512)
    load("scales", scales, sca)
    load("own_codes", codes.at[pl.ds(half, 512)], cod.at[pl.ds(half, 512)])
    load("og", out_grad, og.at[0])
    load("basis", basis, bas)

    def token_columns(q):
        return pl.multiple_of((((z + 1 + q // 2) % 4) * 2 + q % 2) * 1024, 1024)

    def load_tokens(q):
        load(("tok", q), tokens.at[:, pl.ds(token_columns(q), 1024)], tok.at[q % 4])

    for q in range(4):
        load_tokens(q)
    load("other_codes", codes.at[pl.ds(other, 512)], cod.at[pl.ds(other, 512)])
    load("fp", first_prev, fp)
    load("sp", second_prev, sp)

    barrier = pltpu.get_barrier_semaphore()
    for peer in peers:
        pl.semaphore_signal(barrier, inc=1, device_id=peer, device_id_type=MESH)

    def dequantize(base, also):
        def tile(i, carry):
            rows = pl.multiple_of(base + i * 128, 128)
            s = jnp.transpose(sca[:, pl.ds(rows, 128)])
            for g in range(8):
                cols = slice(g * 128, (g + 1) * 128)
                w = (cod[pl.ds(rows, 128), cols].astype(F32) * s[:, g : g + 1]).astype(BF16)
                weight[pl.ds(rows, 128), cols] = w
                if also:
                    W[0, pl.ds(pl.multiple_of(i * 128, 128), 128), cols] = w
            return carry

        lax.fori_loop(0, 4, tile, 0)

    loads["scales"].wait()
    loads["own_codes"].wait()
    dequantize(half, True)

    pl.semaphore_wait(barrier, len(peers))
    net = Net(send_sems, recv_sems)

    def wsend(name, way, dz, h, start, size):
        device, to_dz, to_h = {
            "z+": (zp, (dz + 3) % 4, h),
            "z-": (zm, (dz + 1) % 4, h),
            "xc": (xc, dz, 1 - h),
            "xs": (xs, dz, h),
        }[way]
        if not isinstance(start, int):
            start = pl.multiple_of(start, 64)
        rows = pl.ds(start, size)
        net.start(name, W.at[dz * 2 + h, rows], W.at[to_dz * 2 + to_h, rows], device)

    wsend("zp1a", "z+", 0, 0, 0, 256)
    wsend("zm1a", "z-", 0, 0, 256, 256)
    wsend("xc0", "xc", 0, 0, xlo * 256, 256)
    loads["og"].wait()
    net.start("og", og.at[0], og.at[1], sib)
    wsend("zp1b", "z+", 0, 0, 256, 256)
    wsend("zm1b", "z-", 0, 0, 0, 256)

    loads["basis"].wait()
    projected = jnp.dot(og[0], bas[...], preferred_element_type=F32).astype(BF16)
    turned = jnp.transpose(projected)
    for j in range(16):
        jx, jy, jc = j // 8, (j // 2) % 4, j % 2
        row = jnp.where(c == jc, 0, 256) + ((jy - y + 4) % 4) * 64 + jx * 32
        proj_t[pl.ds(pl.multiple_of(row, 32), 32), :] = turned[j * 32 : (j + 1) * 32, :]

    def partial_sums(q):
        loads["tok", q].wait()

        def tile(i, carry):
            cols = pl.ds(pl.multiple_of(i * 256, 256), 256)
            acc = jnp.dot(proj_t[...], tok[q % 4, :, cols], preferred_element_type=F32)
            own[q % (LAG + 1), :, cols] = acc[:256]
            sib_out[q, :, cols] = acc[256:].astype(BF16)
            return carry

        lax.fori_loop(0, 4, tile, 0)
        net.start(("sib", q), sib_out.at[q], sib_in.at[q], sib)
        if q + 4 < 8:
            load_tokens(q + 4)

    def chip_sums(q):
        net.recv(("sib", q))

        def tile(i, carry):
            rows = pl.ds(pl.multiple_of(i * 64, 64), 64)
            cs[q, rows, :] = (own[q % (LAG + 1), rows, :] + sib_in[q, rows, :].astype(F32)).astype(BF16)
            return carry

        lax.fori_loop(0, 4, tile, 0)
        net.start(("far", q), cs.at[q, pl.ds(128, 64)], rr.at[q], (yp, ym)[q % 2])

    def relay(q):
        net.recv(("far", q))
        near, direct = ((64, 192), (192, 64))[q % 2]
        s2[q] = (cs[q, near : near + 64, :].astype(F32) + rr[q].astype(F32)).astype(BF16)
        net.start(("near", q), s2.at[q], y_in.at[q, q % 2], (yp, ym)[q % 2])
        net.start(("direct", q), cs.at[q, pl.ds(direct, 64)], y_in.at[q, 1 - q % 2], (ym, yp)[q % 2])

    def y_sums(k):
        for h in range(2):
            q = 2 * k + h
            net.recv(("near", q))
            net.recv(("direct", q))
            cs2[k, h] = (cs[q, 0:64, :].astype(F32) + y_in[q, 0].astype(F32) + y_in[q, 1].astype(F32)).astype(BF16)
        for n, (to, xl, xh) in enumerate(((xc, 1 - xlo, 1 - xhi), (xs, 1 - xlo, xhi), (xo, xlo, 1 - xhi))):
            rows = pl.ds(pl.multiple_of(xl * 32, 32), 32)
            net.start(("x", k, n), cs2.at[k, xh, rows], x_in.at[k, n], to)

    def x_sums(k):
        total = cs2[k, xhi, pl.ds(pl.multiple_of(xlo * 32, 32), 32), :].astype(F32)
        for n in range(3):
            net.recv(("x", k, n))
            total = total + x_in[k, n].astype(F32)
        if k < 3:
            z_out[k] = total.astype(BF16)
            net.start(("z", k), z_out.at[k], z_in.at[k], dev(dz=1 + k))
        return total

    def product(dz, h, u):
        slot = dz * 2 + h
        fsdp = ((z + dz) % 4) * 2 + (xhi if h == 0 else 1 - xhi)
        cols = pl.ds(pl.multiple_of(fsdp * 1024 + c * 512 + u * 256, 256), 256)

        def tile(i, carry):
            rows = pl.ds(pl.multiple_of(i * 256, 256), 256)
            w = W[slot, u * 256 : (u + 1) * 256, :]
            mine = lax.dot_general(og[0, rows, :], w, NT, preferred_element_type=F32)
            ig[rows, cols] = mine.astype(BF16)
            theirs = lax.dot_general(og[1, rows, :], w, NT, preferred_element_type=F32)
            stage[slot, u, rows, :] = theirs.astype(BF16)
            return carry

        lax.fori_loop(0, 2, tile, 0)
        net.start(("ig", slot, u), stage.at[slot, u], ig.at[:, cols], sib)

    for q in range(8):
        partial_sums(q)
        if q >= LAG:
            chip_sums(q - LAG)
    for q in range(8 - LAG, 8):
        chip_sums(q)
    for q in range(4):
        relay(q)
    net.recv("og")
    product(0, 0, 0)
    product(0, 0, 1)

    net.recv("zp1a")
    wsend("zp2", "z+", 3, 0, 0, 256)
    wsend("xc3a", "xc", 3, 0, 128 + xlo * 64, 64)
    net.recv("zm1a")
    wsend("zm2", "z-", 1, 0, 256, 256)
    wsend("xc1a", "xc", 1, 0, 256 + xlo * 64, 64)
    net.recv("xc0")
    wsend("xs0", "xs", 0, 1, (1 - xlo) * 256, 256)
    for q in range(4, 8):
        relay(q)
    product(3, 0, 0)
    product(1, 0, 1)
    loads["other_codes"].wait()
    dequantize(other, False)
    y_sums(0)

    net.recv("zp1b")
    wsend("xc3b", "xc", 3, 0, 256 + xlo * 128, 128)
    net.recv("zm1b")
    wsend("xc1b", "xc", 1, 0, xlo * 128, 128)
    net.recv("xc3a")
    wsend("xs3a", "xs", 3, 1, 128 + (1 - xlo) * 64, 64)
    net.recv("xc1a")
    wsend("xs1a", "xs", 1, 1, 256 + (1 - xlo) * 64, 64)
    net.recv("xs0")
    wsend("zp_o1", "z+", 0, 1, 0, 128)
    wsend("zm_o1", "z-", 0, 1, 384, 128)
    x_sums(0)
    product(3, 0, 1)
    product(1, 0, 0)
    product(0, 1, 0)
    product(0, 1, 1)
    y_sums(1)

    net.recv("zp2")
    wsend("xc2a", "xc", 2, 0, 128 + xlo * 64, 64)
    net.recv("zm2")
    wsend("xc2b", "xc", 2, 0, 256 + xlo * 64, 64)
    x_sums(1)
    y_sums(2)
    net.recv("zp_o1")
    wsend("zp_o2", "z+", 3, 1, 0, 128)
    net.recv("zm_o1")
    wsend("zm_o2", "z-", 1, 1, 384, 128)
    net.recv("xc3b")
    wsend("xs3b", "xs", 3, 1, 256 + (1 - xlo) * 128, 128)
    net.recv("xc1b")
    wsend("xs1b", "xs", 1, 1, (1 - xlo) * 128, 128)
    product(2, 0, 0)
    product(2, 0, 1)
    x_sums(2)
    y_sums(3)
    net.recv("xs3a")
    product(3, 1, 0)
    net.recv("xs1a")
    product(1, 1, 1)
    low = x_sums(3)
    for k in range(3):
        net.recv(("z", k))
        low = low + z_in[k].astype(F32)

    loads["fp"].wait()
    loads["sp"].wait()
    first = beta_one * fp[...] + (1.0 - beta_one) * low
    second = beta_two * sp[...] + (1.0 - beta_two) * low * low
    first_new[...] = first
    second_new[...] = second
    mine = pl.ds(pl.multiple_of(d * 32, 32), 32)
    step_all[mine, :] = (first / (jnp.sqrt(second) + epsilon)).astype(BF16)
    for j in range(1, 8):
        net.start(("step", j), step_all.at[mine], step_all.at[mine], dev(dx=j // 4, dy=j % 4))
    net.start(("step_sib", 0), step_all.at[mine], step_all.at[mine], sib)

    net.recv("xc2a")
    wsend("xs2a", "xs", 2, 1, 128 + (1 - xlo) * 64, 64)
    net.recv("xc2b")
    wsend("xs2b", "xs", 2, 1, 256 + (1 - xlo) * 64, 64)
    net.recv("xs3b")
    product(3, 1, 1)
    net.recv("xs1b")
    product(1, 1, 0)
    for j in range(1, 8):
        net.recv(("step", j))
        xl = 1 - xlo if j // 4 else xlo
        rows = pl.ds(pl.multiple_of((xl * 8 + ((y - j % 4 + 4) % 4) * 2 + c) * 32, 32), 32)
        net.start(("step_sib", j), step_all.at[rows], step_all.at[rows], sib)
    net.recv("zp_o2")
    net.recv("xs2a")
    product(2, 1, 0)
    net.recv("zm_o2")
    net.recv("xs2b")
    product(2, 1, 1)
    net.finish()


def write_out(ig, step_all, first_new, second_new, weight, basis, ig_out, first_out, second_out, weight_out, nw, sems):
    copies = [
        pltpu.make_async_copy(ig.at[pl.ds(i * 128, 128)], ig_out.at[pl.ds(i * 128, 128)], sems.at[i]) for i in range(4)
    ]
    copies.append(pltpu.make_async_copy(first_new, first_out, sems.at[4]))
    copies.append(pltpu.make_async_copy(second_new, second_out, sems.at[5]))
    for copy in copies:
        copy.start()
    for i in range(4):
        rows = slice(i * 256, (i + 1) * 256)
        step = jnp.transpose(step_all[:, rows])
        change = lax.dot_general(step, basis[...], NT, preferred_element_type=F32)
        nw[rows, :] = (weight[rows, :].astype(F32) - learn_rate * change).astype(BF16)
        copy = pltpu.make_async_copy(nw.at[pl.ds(i * 256, 256)], weight_out.at[pl.ds(i * 256, 256)], sems.at[6 + i])
        copy.start()
        copies.append(copy)
    for copy in copies:
        copy.wait()


def shards(tokens, out_grad, weight_codes, block_scales, proj_basis, first_prev, second_prev):
    any_spec = pl.BlockSpec(memory_space=pl.ANY)
    vmem_spec = pl.BlockSpec(memory_space=pltpu.VMEM)
    held = pl.pallas_call(
        exchange,
        name="exchange",
        out_shape=(
            pltpu.VMEM((TOK, D), BF16),
            pltpu.VMEM((RANK, 1024), BF16),
            pltpu.VMEM((32, 1024), F32),
            pltpu.VMEM((32, 1024), F32),
            pltpu.VMEM((1024, N), BF16),
        ),
        in_specs=[any_spec] * 7,
        out_specs=(vmem_spec,) * 5,
        scratch_shapes=[
            pltpu.VMEM((8, 512, 1024), BF16),
            pltpu.VMEM((2, 512, 1024), BF16),
            pltpu.VMEM((8, 2, 512, 256), BF16),
            pltpu.VMEM((1024, 1024), BF16),
            pltpu.VMEM((8, 1024), F32),
            pltpu.VMEM((1024, 512), BF16),
            pltpu.VMEM((4, 512, 1024), BF16),
            pltpu.VMEM((512, 512), BF16),
            pltpu.VMEM((8, 256, 1024), BF16),
            pltpu.VMEM((8, 256, 1024), BF16),
            pltpu.VMEM((LAG + 1, 256, 1024), F32),
            pltpu.VMEM((8, 256, 1024), BF16),
            pltpu.VMEM((8, 64, 1024), BF16),
            pltpu.VMEM((8, 64, 1024), BF16),
            pltpu.VMEM((8, 2, 64, 1024), BF16),
            pltpu.VMEM((4, 2, 64, 1024), BF16),
            pltpu.VMEM((4, 3, 32, 1024), BF16),
            pltpu.VMEM((3, 32, 1024), BF16),
            pltpu.VMEM((3, 32, 1024), BF16),
            pltpu.VMEM((32, 1024), F32),
            pltpu.VMEM((32, 1024), F32),
            pltpu.SemaphoreType.DMA((COPIES,)),
            pltpu.SemaphoreType.DMA((COPIES,)),
            pltpu.SemaphoreType.DMA((16,)),
        ],
        compiler_params=pltpu.CompilerParams(
            collective_id=0, has_side_effects=True, vmem_limit_bytes=50 * 2**20
        ),
        cost_estimate=pl.CostEstimate(flops=14 * 10**9, bytes_accessed=13 * 2**20, transcendentals=0),
    )(tokens, out_grad, weight_codes, block_scales.T, proj_basis, first_prev.T, second_prev.T)
    ig, first, second, weight = pl.pallas_call(
        write_out,
        name="write_out",
        out_shape=(
            jax.ShapeDtypeStruct((TOK, D), BF16),
            jax.ShapeDtypeStruct((32, 1024), F32),
            jax.ShapeDtypeStruct((32, 1024), F32),
            jax.ShapeDtypeStruct((1024, N), BF16),
        ),
        in_specs=[vmem_spec] * 6,
        out_specs=(any_spec,) * 4,
        scratch_shapes=[pltpu.VMEM((1024, 1024), BF16), pltpu.SemaphoreType.DMA((10,))],
        compiler_params=pltpu.CompilerParams(vmem_limit_bytes=16 * 2**20),
        cost_estimate=pl.CostEstimate(flops=10**9, bytes_accessed=14 * 2**20, transcendentals=0),
    )(*held, proj_basis)
    return ig, first.T, second.T, weight


def solution(mesh):
    in_specs = (
        P(("dp", "fsdp"), None),
        P(("dp", "fsdp"), None),
        P("fsdp", None),
        P("fsdp", None),
        P(),
        P("fsdp", "dp"),
        P("fsdp", "dp"),
    )
    out_specs = (P(("dp", "fsdp"), None), P("fsdp", "dp"), P("fsdp", "dp"), P("fsdp", None))
    return jax.shard_map(shards, mesh=mesh, in_specs=in_specs, out_specs=out_specs, check_vma=False)
```

time: 425 us -> 88.5 us (0.21)
  waiting for transfers between devices: 360 us -> 0 us
  Pallas kernels: 0 us -> 87.8 us
  matrix products: 32 us -> 0 us
  local copies, waits for them, and re-layouts: 14.9 us -> 0.01 us
  between operations: 13.8 us -> 0.66 us
    all_gather x2 -> x0, waiting for transfers between devices: 211 us -> none  [the longest x1 181 us: shards(): lax.all_gather(weight, 'fsdp', axis=0, tiled=True)]
    reduce_scatter x2 -> x0, waiting for transfers between devices: 149 us -> none  [the longest x1 74.9 us: shards(): lax.psum_scatter(col_shares, 'fsdp', scatter_dimension=0, tiled=True)]
    pallas_call x0 -> x2, Pallas kernels: none -> 87.8 us  [the longest x1 83.7 us: shards(): pl.pallas_call(exchange, name='exchange', out_shape=(pltpu.VMEM((TOK, D),...]
    dot_general x3 -> x0, matrix products: 32 us -> none  [the longest x1 16.9 us: shards(): lax.dot_general(out_grad, lax.all_gather(weight, 'fsdp', axis=0, tiled=Tr...]
    unnamed x14 -> x2, local copies, waits for them, and re-layouts: 13.7 us -> 0.01 us
  transfers between devices with their start and end apart: 4 -> 0, of which waited for: 4 -> 0; matrix products, arithmetic and copies ran while one was open for 2% -> 0% of each run, Pallas kernels for 0% -> 0%
where the time goes in v1:
time: 88.5 us; the launch traced here: 88.4 us
  Pallas kernels  87.8 us (99%)
    pallas_call x1, Pallas kernels, shards(): pl.pallas_call(exchange, name='exchange', out_shape=(pltpu.VMEM((TOK, D),...  83.7 us
    pallas_call x1, Pallas kernels, shards(): pl.pallas_call(write_out, name='write_out', out_shape=(jax.ShapeDtypeStru...  4.08 us

profile of v1, /device:TPU:1, one launch (start us, length us, event | category | flops | bytes accessed | tf_op | source)
XLA Modules:
  0.0 88.4 jit_solution(18130931218460488741)
XLA Ops:
  0.6 0.0 copy-start
  0.6 83.7 %exchange.1 = (bf16[512,8192]{1,0:T(8,128)(2,1)S(1)}, bf16[512,1024]{1,0:T(8,128)(2,1)S(1)}, f32[32,1024]{1,0:T(8,128)S(1)}, f32[32,1024]{1,0:T(8,128)S(1)}, bf16[1024,1024]{1,0:T(8,128)(2,1)S(1)}) custom-call(bf16[512,8192]{1,0:T(8,128)(2,1)} %tokens.1, bf16[512,1024]{1,0:T(8,128)(2,1)} %out_grad.1, bf16[1024,1024]{1,0:T(8,128)(2,1)} %codes.1, ...), custom_call_target="tpu_custom_call" | custom-call | flops 14000000000 | bytes 13631488 | tf_op jit(solution)/shard_map/exchange/pallas_call | solution.py:362
  84.3 0.0 copy-done
  84.3 4.1 %write_out.1 = (bf16[512,8192]{1,0:T(8,128)(2,1)}, f32[32,1024]{1,0:T(8,128)}, f32[32,1024]{1,0:T(8,128)}, bf16[1024,1024]{1,0:T(8,128)(2,1)}) custom-call(bf16[512,8192]{1,0:T(8,128)(2,1)S(1)} %get-tuple-element.13.ig, bf16[512,1024]{1,0:T(8,128)(2,1)S(1)} %get-tuple-element.14.step_all, f32[32,1024]{1,0:T(8,128)S(1)} %get-tuple-element.15.first_new, ...), custom_call_target="tpu_custom_call" | custom-call | flops 1000000000 | bytes 14680064 | tf_op jit(solution)/shard_map/write_out/pallas_call | solution.py:405
Async XLA Ops:
  0.6 83.7 %copy-start = (bf16[1024,512]{1,0:T(8,128)(2,1)S(1)}, bf16[1024,512]{1,0:T(8,128)(2,1)}, u32[]{:S(2)}) copy-start(bf16[1024,512]{1,0:T(8,128)(2,1)} %basis.3) | copy-start | bytes 3145732

commit v2 on v1

v2 whole, which is shorter than its diff:
```python
import math

import jax
import jax.numpy as jnp
from jax import lax
from jax.experimental import pallas as pl
from jax.experimental.pallas import tpu as pltpu
from jax.sharding import PartitionSpec as P

MESH = pl.DeviceIdType.MESH
BF16 = jnp.bfloat16
F32 = jnp.float32
beta_one = 0.9
beta_two = 0.999
learn_rate = 0.2
epsilon = 1e-08

D = 8192
N = 1024
RANK = 512
TOK = 512
OWN = 3
CHUNKS = ((1, 0, 1024), (2, 0, 1024), (3, 0, 1024), (0, 0, 512), (0, 512, 512))
OWN_AT = 3
ORDER = (
    ("P", 0), ("W0b",), ("P", 1), ("P", 2), ("M", 0, 0, 1), ("C", 0), ("E", 0), ("P", 3), ("C", 1), ("P", 4),
    ("C", 2), ("E", 1), ("E", 2), ("Fxc0", 0), ("P", 5), ("M", 0, 0, 0), ("C", 3), ("P", 6), ("C", 4), ("P", 7),
    ("Fxc0", 3), ("E", 3), ("E", 4), ("D2",), ("R", 0), ("C", 5), ("P", 8), ("C", 6), ("C", 7), ("E", 6), ("E", 7),
    ("E", 5), ("P", 9), ("Fxc0", 1), ("R", 2), ("R", 1), ("C", 8), ("E", 8), ("Fzp", 1), ("M", 3, 0, 0), ("C", 9),
    ("E", 9), ("M", 1, 0, 1), ("Fxc0", 2), ("Fzm", 2), ("M", 0, 1, 0), ("Fxc3", 1), ("R", 4), ("R", 3), ("Fzm", 1),
    ("Fzp", 0), ("Fzp", 2), ("M", 0, 1, 1), ("Fxc1", 2), ("Y", 0), ("R", 5), ("Fzm", 3), ("Fzp", 3), ("M", 3, 0, 1),
    ("R", 7), ("Fxc1", 1), ("R", 6), ("M", 1, 0, 0), ("Fxc3", 2), ("Fo1", 3), ("Y", 1), ("F2", 1), ("Y", 2), ("R", 9),
    ("R", 8), ("Fxc3", 3), ("X", 0), ("Y", 3), ("M", 2, 0, 1), ("M", 2, 0, 0), ("Fo3", 0), ("Y", 4), ("Y", 5),
    ("M", 3, 1, 1), ("Y", 7), ("Y", 6), ("X", 1), ("Y", 8), ("Y", 9), ("Fzm", 0), ("M", 1, 1, 1), ("X", 2), ("F2", 2),
    ("Fxc2", 1), ("X", 3), ("Fr3", 0), ("M", 3, 1, 0), ("Fr1", 3), ("X", 4), ("U", 1), ("U", 0), ("Fxc1", 0),
    ("T", 1), ("T", 0), ("Fxc2", 2), ("M", 2, 1, 0), ("S", 1), ("M", 1, 1, 0), ("S", 0), ("M", 2, 1, 1),
)
NT = (((1,), (1,)), ((), ()))


class Net:
    def __init__(self, send_sems, recv_sems, rows):
        self.send_sems, self.recv_sems, self.rows = send_sems, recv_sems, rows
        self.sems, self.got, self.sent = {}, set(), [0]

    def start(self, name, src, dst, device):
        size = math.prod(dst.shape) // N
        if self.sent[-1] + size > self.rows.shape[0]:
            self.sent.append(0)
        self.sent[-1] += size
        at, copies = self.sems.setdefault(name, (len(self.sems), []))
        copy = pltpu.make_async_remote_copy(
            src_ref=src,
            dst_ref=dst,
            send_sem=self.send_sems.at[len(self.sent) - 1],
            recv_sem=self.recv_sems.at[at],
            device_id=device,
            device_id_type=MESH,
        )
        copy.start()
        copies.append(size)

    def recv(self, name):
        if name not in self.got:
            self.got.add(name)
            at, copies = self.sems[name]
            whole = self.rows.at[: sum(copies)]
            pltpu.make_async_copy(whole, whole, self.recv_sems.at[at]).wait()

    def finish(self):
        for name in self.sems:
            self.recv(name)
        for at, size in enumerate(self.sent):
            whole = self.rows.at[:size]
            pltpu.make_async_copy(whole, whole, self.send_sems.at[at]).wait()


RECV_SEMS = 90
SEND_SEMS = 3


def exchange(
    tokens, out_grad, codes, scales, basis, first_prev, second_prev,
    ig, step_all, first_new, second_new, weight,
    W, og, stage, cod, sca, bas, tok, proj_t, sib_out, sib_in, own, cs, rr, s2, y_in, cs2, x_in, low, z_out, z_in,
    fp, sp, send_sems, recv_sems, load_sems,
):
    d = lax.axis_index("dp")
    f = lax.axis_index("fsdp")
    xlo, y, c = d // 8, (d // 2) % 4, d % 2
    z, xhi = f // 2, f % 2

    def dev(dx=0, dh=0, dy=0, dz=0, dc=0):
        xl = 1 - xlo if dx else xlo
        xh = 1 - xhi if dh else xhi
        cc = 1 - c if dc else c
        return (xl * 8 + ((y + dy) % 4) * 2 + cc, ((z + dz) % 4) * 2 + xh)

    sib = dev(dc=1)
    zp, zm = dev(dz=1), dev(dz=3)
    yp, ym = dev(dy=1), dev(dy=3)
    xc, xs, xo = dev(dx=1, dh=1), dev(dx=1), dev(dh=1)
    peers = [sib, zp, zm, dev(dz=2), xc, xs, xo] + [dev(dx=j // 4, dy=j % 4) for j in (1, 2, 3, 5, 6, 7)]

    loads = {}

    def load(name, src, dst):
        copy = pltpu.make_async_copy(src, dst, load_sems.at[len(loads)])
        loads[name] = copy
        copy.start()

    half = pl.multiple_of(c * 512, 512)
    other = pl.multiple_of(512 - c * 512, 512)
    load("scales", scales, sca)
    load("own_codes", codes.at[pl.ds(half, 512)], cod.at[pl.ds(half, 512)])
    load("og", out_grad, og.at[0])
    load("basis", basis, bas)

    def part(q):
        dz, at, width = CHUNKS[q // 2]
        h = 1 - q % 2
        return dz, h, ((dz + 3) % 4) * 2 + h, slice(at, at + width), width

    def load_tokens(q):
        dz, h, _, cols, width = part(q)
        at = (((z + dz) % 4) * 2 + (1 - xhi if h else xhi)) * 1024 + cols.start
        src = tokens.at[:, pl.ds(pl.multiple_of(at, 512), width)]
        load(("tok", q), src, tok.at[q % 4, :, :width])

    for q in range(4):
        load_tokens(q)
    load("other_codes", codes.at[pl.ds(other, 512)], cod.at[pl.ds(other, 512)])
    load("fp", first_prev, fp)
    load("sp", second_prev, sp)

    barrier = pltpu.get_barrier_semaphore()
    for peer in peers:
        pl.semaphore_signal(barrier, inc=1, device_id=peer, device_id_type=MESH)

    def dequantize(base, tiles, also):
        for i in tiles:
            rows = pl.ds(pl.multiple_of(base + i * 128, 128), 128)
            s = jnp.transpose(sca[:, rows])
            for g in range(8):
                cols = slice(g * 128, (g + 1) * 128)
                w = (cod[rows, cols].astype(F32) * s[:, g : g + 1]).astype(BF16)
                weight[rows, cols] = w
                if also:
                    W[i * 128 : (i + 1) * 128, cols] = w

    loads["scales"].wait()
    loads["own_codes"].wait()
    dequantize(half, (0, 3), True)
    pl.semaphore_wait(barrier, len(peers))
    net = Net(send_sems, recv_sems, W)

    def half_of(i, xl):
        return i * 128 + xl * 64

    def wsend(name, way, dz, h, start, size):
        device, to_dz, to_h = {
            "z+": (zp, (dz + 3) % 4, h),
            "z-": (zm, (dz + 1) % 4, h),
            "xc": (xc, dz, 1 - h),
            "xs": (xs, dz, h),
        }[way]
        src, dst = ((dz * 2 + h) * 512 + start, (to_dz * 2 + to_h) * 512 + start)
        if not isinstance(start, int):
            src, dst = pl.multiple_of(src, 32), pl.multiple_of(dst, 32)
        net.start(name, W.at[pl.ds(src, size)], W.at[pl.ds(dst, size)], device)

    wsend(("zp", 0), "z+", 0, 0, 0, 128)
    wsend(("zm", 3), "z-", 0, 0, 384, 128)
    wsend(("xc0", 0), "xc", 0, 0, half_of(0, xlo), 64)
    wsend(("xc0", 3), "xc", 0, 0, half_of(3, xlo), 64)

    loads["og"].wait()
    loads["basis"].wait()
    projected = jnp.dot(og[0], bas[...], preferred_element_type=F32).astype(BF16)
    turned = jnp.transpose(projected)
    for j in range(16):
        jx, jy, jc = j // 8, (j // 2) % 4, j % 2
        row = jnp.where(c == jc, 0, 256) + ((jy - y + 4) % 4) * 64 + jx * 32
        proj_t[pl.ds(pl.multiple_of(row, 32), 32), :] = turned[j * 32 : (j + 1) * 32, :]

    def multiply(q):
        _, _, slot, span, width = part(q)
        loads["tok", q].wait()

        for i in range(0, width, 256):
            acc = jnp.dot(proj_t[...], tok[q % 4, :, i : i + 256], preferred_element_type=F32)
            own[q % OWN, :, i : i + 256] = acc[:256]
            sib_out[slot, :, span.start + i : span.start + i + 256] = acc[256:].astype(BF16)
        if q + 4 < 2 * len(CHUNKS):
            load_tokens(q + 4)

    def P(q):
        _, _, slot, cols, _ = part(q)
        multiply(q)
        if q == 0:
            net.start(("og",), og.at[0], og.at[1], sib)
        net.start(("sib", q), sib_out.at[slot, :, cols], sib_in.at[slot, :, cols], sib)

    def C(q):
        _, h, slot, cols, width = part(q)
        net.recv(("sib", q))

        def tile(i, carry):
            rows = pl.ds(pl.multiple_of(i * 64, 64), 64)
            total = own[q % OWN, rows, :width] + sib_in[slot, rows, cols].astype(F32)
            cs[slot, rows, cols] = total.astype(BF16)
            return carry

        lax.fori_loop(0, 4, tile, 0)
        net.start(("far", q), cs.at[slot, 128:192, cols], rr.at[slot, :, cols], yp if h else ym)

    def E(q):
        _, h, slot, cols, _ = part(q)
        rows = slice(192, 256) if h else slice(64, 128)
        net.start(("y", q), cs.at[slot, rows, cols], y_in.at[slot, h, :, cols], ym if h else yp)

    def R(q):
        _, h, slot, cols, _ = part(q)
        net.recv(("far", q))
        rows = slice(64, 128) if h else slice(192, 256)
        s2[slot, :, cols] = (cs[slot, rows, cols].astype(F32) + rr[slot, :, cols].astype(F32)).astype(BF16)
        net.start(("y", q), s2.at[slot, :, cols], y_in.at[slot, 1 - h, :, cols], yp if h else ym)

    def Y(q):
        _, h, slot, cols, _ = part(q)
        net.recv(("y", q))
        total = cs[slot, 0:64, cols].astype(F32) + y_in[slot, 0, :, cols].astype(F32)
        cs2[slot, :, cols] = (total + y_in[slot, 1, :, cols].astype(F32)).astype(BF16)
        for n, to, xl in ((0, xc, 1 - xlo), (2, xo, xlo)) if h else ((1, xs, 1 - xlo),):
            rows = pl.ds(pl.multiple_of(xl * 32, 32), 32)
            net.start(("x", q // 2), cs2.at[slot, rows, cols], x_in.at[slot // 2, n, :, cols], to)

    def X(k):
        dz, _, slot, cols, _ = part(2 * k + 1)
        total = cs2[slot, pl.ds(pl.multiple_of(xlo * 32, 32), 32), cols].astype(F32)
        net.recv(("x", k))
        for n in range(3):
            total = total + x_in[slot // 2, n, :, cols].astype(F32)
        if dz == 0:
            low[:, cols] = total
        else:
            z_out[dz - 1] = total.astype(BF16)
            net.start(("z",), z_out.at[dz - 1], z_in.at[dz - 1], dev(dz=dz))

    def U(j):
        cols = part(2 * OWN_AT + 2 * j)[3]
        total = low[:, cols]
        net.recv(("z",))
        for dz in (1, 2, 3):
            total = total + z_in[dz - 1, :, cols].astype(F32)
        for name in ("fp", "sp"):
            if name in loads:
                loads.pop(name).wait()
        first = beta_one * fp[:, cols] + (1.0 - beta_one) * total
        second = beta_two * sp[:, cols] + (1.0 - beta_two) * total * total
        first_new[:, cols] = first
        second_new[:, cols] = second
        step_all[xlo * 4 + y, c, :, cols] = (first / (jnp.sqrt(second) + epsilon)).astype(BF16)
        mine = step_all.at[xlo * 4 + y, c, :, cols]
        net.start(("sx", j), mine, mine, xs)
        for i in (1, 3, 2):
            net.start(("step", j), mine, mine, dev(dy=i))

    def T(j):
        cols = part(2 * OWN_AT + 2 * j)[3]
        net.recv(("sx", j))
        theirs = step_all.at[(1 - xlo) * 4 + y, c, :, cols]
        for i in (1, 3, 2):
            net.start(("step", j), theirs, theirs, dev(dy=i))

    def S(j):
        cols = part(2 * OWN_AT + 2 * j)[3]
        net.recv(("step", j))
        ours = step_all.at[:, c, :, cols]
        net.start(("ss",), ours, ours, sib)

    def D2():
        loads["other_codes"].wait()
        dequantize(other, range(4), False)

    def Fzp(i):
        net.recv(("zp", i))
        if i < 2:
            wsend(("zpp", i), "z+", 3, 0, i * 128, 128)
        if i != 0:
            wsend(("xc3", i), "xc", 3, 0, half_of(i, xlo), 64)

    def Fzm(i):
        net.recv(("zm", i))
        if i >= 2:
            wsend(("zmm", i), "z-", 1, 0, i * 128, 128)
        if i != 3:
            wsend(("xc1", i), "xc", 1, 0, half_of(i, xlo), 64)

    def forward_x(dz):
        def run(i):
            net.recv(("xc%d" % dz, i))
            wsend(("xs%d" % dz, i), "xs", dz, 1, half_of(i, 1 - xlo), 64)

        return run

    def Fo3(i):
        net.recv(("xc0", i))
        net.recv(("xs0", i))
        wsend(("zo3", i), "z+", 0, 1, i * 128, 128)

    def Fo1(i):
        net.recv(("xc0", i))
        net.recv(("xs0", i))
        wsend(("zo1", i), "z-", 0, 1, i * 128, 128)

    def Fr3(i):
        net.recv(("zo3", i))
        wsend(("zr3", i), "z+", 3, 1, i * 128, 128)

    def Fr1(i):
        net.recv(("zo1", i))
        wsend(("zr1", i), "z-", 1, 1, i * 128, 128)

    def F2(i):
        net.recv(("zpp", i) if i < 2 else ("zmm", i))
        wsend(("xc2", i), "xc", 2, 0, half_of(i, xlo), 64)

    def M(dz, h, u):
        for i in (2 * u, 2 * u + 1):
            if h == 0:
                if dz:
                    net.recv((None, "zm", "zpp" if i < 2 else "zmm", "zp")[dz : dz + 1] + (i,))
            elif (dz, i) in ((3, 0), (1, 3)):
                net.recv(("zo%d" % dz, i))
            elif dz == 2 and i in (0, 3):
                net.recv(("zr%d" % (1 if i else 3), i))
            else:
                net.recv(("xc%d" % dz, i))
                net.recv(("xs%d" % dz, i))
        net.recv(("og",))
        slot = dz * 2 + h
        fsdp = ((z + dz) % 4) * 2 + (1 - xhi if h else xhi)
        cols = pl.ds(pl.multiple_of(fsdp * 1024 + c * 512 + u * 256, 256), 256)

        at = slot * 512 + u * 256

        def tile(i, carry):
            rows = pl.ds(pl.multiple_of(i * 256, 256), 256)
            w = W[at : at + 256, :]
            theirs = lax.dot_general(og[1, rows, :], w, NT, preferred_element_type=F32)
            stage[slot, u, rows, :] = theirs.astype(BF16)
            mine = lax.dot_general(og[0, rows, :], w, NT, preferred_element_type=F32)
            ig[rows, cols] = mine.astype(BF16)
            return carry

        lax.fori_loop(0, 2, tile, 0)
        net.start(("ig",), stage.at[slot, u], ig.at[:, cols], sib)

    def W0b():
        dequantize(half, (1, 2), True)
        wsend(("zp", 1), "z+", 0, 0, 128, 128)
        wsend(("zm", 2), "z-", 0, 0, 256, 128)
        wsend(("xc0", 1), "xc", 0, 0, half_of(1, xlo), 64)
        wsend(("xc0", 2), "xc", 0, 0, half_of(2, xlo), 64)
        wsend(("zp", 2), "z+", 0, 0, 256, 128)
        wsend(("zm", 1), "z-", 0, 0, 128, 128)
        wsend(("zp", 3), "z+", 0, 0, 384, 128)
        wsend(("zm", 0), "z-", 0, 0, 0, 128)

    steps = dict(
        W0b=W0b,
        P=P, C=C, E=E, R=R, Y=Y, X=X, U=U, T=T, S=S, M=M, D2=D2, Fzp=Fzp, Fzm=Fzm, Fo3=Fo3, Fo1=Fo1, Fr3=Fr3,
        Fr1=Fr1, F2=F2, Fxc0=forward_x(0), Fxc1=forward_x(1), Fxc2=forward_x(2), Fxc3=forward_x(3),
    )
    for name, *place in ORDER:
        steps[name](*place)
    net.finish()


def write_out(ig, step_all, first_new, second_new, weight, basis, ig_out, first_out, second_out, weight_out, nw, sems):
    copies = [
        pltpu.make_async_copy(ig.at[pl.ds(i * 128, 128)], ig_out.at[pl.ds(i * 128, 128)], sems.at[i]) for i in range(4)
    ]
    copies.append(pltpu.make_async_copy(first_new, first_out, sems.at[4]))
    copies.append(pltpu.make_async_copy(second_new, second_out, sems.at[5]))
    for copy in copies:
        copy.start()
    for i in range(4):
        rows = slice(i * 256, (i + 1) * 256)
        step = jnp.transpose(step_all[:, :, :, rows].reshape(RANK, 256))
        change = lax.dot_general(step, basis[...], NT, preferred_element_type=F32)
        nw[rows, :] = (weight[rows, :].astype(F32) - learn_rate * change).astype(BF16)
        copy = pltpu.make_async_copy(nw.at[pl.ds(i * 256, 256)], weight_out.at[pl.ds(i * 256, 256)], sems.at[6 + i])
        copy.start()
        copies.append(copy)
    for copy in copies:
        copy.wait()


def shards(tokens, out_grad, weight_codes, block_scales, proj_basis, first_prev, second_prev):
    any_spec = pl.BlockSpec(memory_space=pl.ANY)
    vmem_spec = pl.BlockSpec(memory_space=pltpu.VMEM)
    held = pl.pallas_call(
        exchange,
        name="exchange",
        out_shape=(
            pltpu.VMEM((TOK, D), BF16),
            pltpu.VMEM((8, 2, 32, 1024), BF16),
            pltpu.VMEM((32, 1024), F32),
            pltpu.VMEM((32, 1024), F32),
            pltpu.VMEM((1024, N), BF16),
        ),
        in_specs=[any_spec] * 7,
        out_specs=(vmem_spec,) * 5,
        scratch_shapes=[
            pltpu.VMEM((4096, 1024), BF16),
            pltpu.VMEM((2, 512, 1024), BF16),
            pltpu.VMEM((8, 2, 512, 256), BF16),
            pltpu.VMEM((1024, 1024), BF16),
            pltpu.VMEM((8, 1024), F32),
            pltpu.VMEM((1024, 512), BF16),
            pltpu.VMEM((4, 512, 1024), BF16),
            pltpu.VMEM((512, 512), BF16),
            pltpu.VMEM((8, 256, 1024), BF16),
            pltpu.VMEM((8, 256, 1024), BF16),
            pltpu.VMEM((OWN, 256, 1024), F32),
            pltpu.VMEM((8, 256, 1024), BF16),
            pltpu.VMEM((8, 64, 1024), BF16),
            pltpu.VMEM((8, 64, 1024), BF16),
            pltpu.VMEM((8, 2, 64, 1024), BF16),
            pltpu.VMEM((8, 64, 1024), BF16),
            pltpu.VMEM((4, 3, 32, 1024), BF16),
            pltpu.VMEM((32, 1024), F32),
            pltpu.VMEM((3, 32, 1024), BF16),
            pltpu.VMEM((3, 32, 1024), BF16),
            pltpu.VMEM((32, 1024), F32),
            pltpu.VMEM((32, 1024), F32),
            pltpu.SemaphoreType.DMA((SEND_SEMS,)),
            pltpu.SemaphoreType.DMA((RECV_SEMS,)),
            pltpu.SemaphoreType.DMA((17,)),
        ],
        compiler_params=pltpu.CompilerParams(
            collective_id=0, has_side_effects=True, vmem_limit_bytes=50 * 2**20
        ),
        cost_estimate=pl.CostEstimate(flops=14 * 10**9, bytes_accessed=13 * 2**20, transcendentals=0),
    )(tokens, out_grad, weight_codes, block_scales.T, proj_basis, first_prev.T, second_prev.T)
    ig, first, second, weight = pl.pallas_call(
        write_out,
        name="write_out",
        out_shape=(
            jax.ShapeDtypeStruct((TOK, D), BF16),
            jax.ShapeDtypeStruct((32, 1024), F32),
            jax.ShapeDtypeStruct((32, 1024), F32),
            jax.ShapeDtypeStruct((1024, N), BF16),
        ),
        in_specs=[vmem_spec] * 6,
        out_specs=(any_spec,) * 4,
        scratch_shapes=[pltpu.VMEM((1024, 1024), BF16), pltpu.SemaphoreType.DMA((10,))],
        compiler_params=pltpu.CompilerParams(vmem_limit_bytes=16 * 2**20),
        cost_estimate=pl.CostEstimate(flops=10**9, bytes_accessed=14 * 2**20, transcendentals=0),
    )(*held, proj_basis)
    return ig, first.T, second.T, weight


def solution(mesh):
    in_specs = (
        P(("dp", "fsdp"), None),
        P(("dp", "fsdp"), None),
        P("fsdp", None),
        P("fsdp", None),
        P(),
        P("fsdp", "dp"),
        P("fsdp", "dp"),
    )
    out_specs = (P(("dp", "fsdp"), None), P("fsdp", "dp"), P("fsdp", "dp"), P("fsdp", None))
    return jax.shard_map(shards, mesh=mesh, in_specs=in_specs, out_specs=out_specs, check_vma=False)
```

time: 88.5 us -> 72.8 us (0.82)
  Pallas kernels: 87.8 us -> 71.9 us
    pallas_call x1, Pallas kernels: 83.7 us -> 67.8 us  [shards(): pl.pallas_call(exchange, name='exchange', out_shape=(pltpu.VMEM((TOK, D),...]
where the time goes in v2:
time: 72.8 us; the launch traced here: 72.7 us
  Pallas kernels  71.9 us (99%)
  between operations  0.82 us (1%)
    pallas_call x1, Pallas kernels, shards(): pl.pallas_call(exchange, name='exchange', out_shape=(pltpu.VMEM((TOK, D),...  67.8 us
    pallas_call x1, Pallas kernels, shards(): pl.pallas_call(write_out, name='write_out', out_shape=(jax.ShapeDtypeStru...  4.08 us

profile of v2, /device:TPU:1, one launch (start us, length us, event | category | flops | bytes accessed | tf_op | source)
XLA Modules:
  0.0 72.7 jit_solution(5419302918403188021)
XLA Ops:
  0.6 0.0 copy-start
  0.6 67.8 %exchange.1 = (bf16[512,8192]{1,0:T(8,128)(2,1)S(1)}, bf16[8,2,32,1024]{3,2,1,0:T(8,128)(2,1)S(1)}, f32[32,1024]{1,0:T(8,128)S(1)}, f32[32,1024]{1,0:T(8,128)S(1)}, bf16[1024,1024]{1,0:T(8,128)(2,1)S(1)}) custom-call(bf16[512,8192]{1,0:T(8,128)(2,1)} %tokens.1, bf16[512,1024]{1,0:T(8,128)(2,1)} %out_grad.1, bf16[1024,1024]{1,0:T(8,128)(2,1)} %codes.1, ...), custom_call_target="tpu_custom_call" | custom-call | flops 14000000000 | bytes 13631488 | tf_op jit(solution)/shard_map/exchange/pallas_call | solution.py:404
  68.5 0.0 copy-done
  68.5 4.1 %write_out.1 = (bf16[512,8192]{1,0:T(8,128)(2,1)}, f32[32,1024]{1,0:T(8,128)}, f32[32,1024]{1,0:T(8,128)}, bf16[1024,1024]{1,0:T(8,128)(2,1)}) custom-call(bf16[512,8192]{1,0:T(8,128)(2,1)S(1)} %get-tuple-element.13.ig, bf16[8,2,32,1024]{3,2,1,0:T(8,128)(2,1)S(1)} %get-tuple-element.14.step_all, f32[32,1024]{1,0:T(8,128)S(1)} %get-tuple-element.15.first_new, ...), custom_call_target="tpu_custom_call" | custom-call | flops 1000000000 | bytes 14680064 | tf_op jit(solution)/shard_map/write_out/pallas_call | solution.py:448
Async XLA Ops:
  0.6 67.8 %copy-start = (bf16[1024,512]{1,0:T(8,128)(2,1)S(1)}, bf16[1024,512]{1,0:T(8,128)(2,1)}, u32[]{:S(2)}) copy-start(bf16[1024,512]{1,0:T(8,128)(2,1)} %basis.3) | copy-start | bytes 3145732

commit v3 on v2

--- a/solution.py
+++ b/solution.py
@@ -23,19 +23,21 @@
 CHUNKS = ((1, 0, 1024), (2, 0, 1024), (3, 0, 1024), (0, 0, 512), (0, 512, 512))
 OWN_AT = 3
 ORDER = (
-    ("P", 0), ("W0b",), ("P", 1), ("P", 2), ("M", 0, 0, 1), ("C", 0), ("E", 0), ("P", 3), ("C", 1), ("P", 4),
-    ("C", 2), ("E", 1), ("E", 2), ("Fxc0", 0), ("P", 5), ("M", 0, 0, 0), ("C", 3), ("P", 6), ("C", 4), ("P", 7),
-    ("Fxc0", 3), ("E", 3), ("E", 4), ("D2",), ("R", 0), ("C", 5), ("P", 8), ("C", 6), ("C", 7), ("E", 6), ("E", 7),
-    ("E", 5), ("P", 9), ("Fxc0", 1), ("R", 2), ("R", 1), ("C", 8), ("E", 8), ("Fzp", 1), ("M", 3, 0, 0), ("C", 9),
-    ("E", 9), ("M", 1, 0, 1), ("Fxc0", 2), ("Fzm", 2), ("M", 0, 1, 0), ("Fxc3", 1), ("R", 4), ("R", 3), ("Fzm", 1),
-    ("Fzp", 0), ("Fzp", 2), ("M", 0, 1, 1), ("Fxc1", 2), ("Y", 0), ("R", 5), ("Fzm", 3), ("Fzp", 3), ("M", 3, 0, 1),
-    ("R", 7), ("Fxc1", 1), ("R", 6), ("M", 1, 0, 0), ("Fxc3", 2), ("Fo1", 3), ("Y", 1), ("F2", 1), ("Y", 2), ("R", 9),
-    ("R", 8), ("Fxc3", 3), ("X", 0), ("Y", 3), ("M", 2, 0, 1), ("M", 2, 0, 0), ("Fo3", 0), ("Y", 4), ("Y", 5),
-    ("M", 3, 1, 1), ("Y", 7), ("Y", 6), ("X", 1), ("Y", 8), ("Y", 9), ("Fzm", 0), ("M", 1, 1, 1), ("X", 2), ("F2", 2),
-    ("Fxc2", 1), ("X", 3), ("Fr3", 0), ("M", 3, 1, 0), ("Fr1", 3), ("X", 4), ("U", 1), ("U", 0), ("Fxc1", 0),
-    ("T", 1), ("T", 0), ("Fxc2", 2), ("M", 2, 1, 0), ("S", 1), ("M", 1, 1, 0), ("S", 0), ("M", 2, 1, 1),
+    ("P", 0), ("W0b",), ("P", 1), ("P", 2), ("C", 0), ("C", 1), ("C", 2), ("E", 0), ("P", 3), ("Fxc0", 0), ("P", 4),
+    ("M", 0, 0, 0), ("Fxc0", 3), ("C", 3), ("P", 5), ("P", 6), ("Fxc0", 1), ("E", 2), ("C", 4), ("M", 0, 0, 1),
+    ("R", 0), ("C", 5), ("Fzm", 2), ("E", 1), ("E", 3), ("P", 7), ("Fxc0", 2), ("Fzp", 1), ("Fxc1", 2), ("R", 1),
+    ("Fzm", 1), ("R", 3), ("P", 8), ("Y", 0), ("M", 3, 0, 0), ("C", 6), ("E", 5), ("M", 0, 1, 0), ("R", 5), ("C", 8),
+    ("P", 9), ("R", 2), ("Fxc3", 1), ("Fzm", 0), ("Fo3", 0), ("Fxc1", 1), ("Fo1", 3), ("M", 1, 0, 1), ("R", 4),
+    ("C", 7), ("Fzp", 3), ("Y", 1), ("R", 6), ("E", 4), ("Y", 3), ("M", 1, 0, 0), ("F2", 1), ("Fzp", 0),
+    ("M", 0, 1, 1), ("Fxc1", 0), ("E", 6), ("F2", 2), ("Y", 5), ("C", 9), ("D2",), ("Y", 2), ("R", 8), ("R", 7),
+    ("Fr3", 0), ("Fxc2", 1), ("Fr1", 3), ("E", 7), ("X", 0), ("E", 9), ("Y", 4), ("E", 8), ("Fxc2", 2),
+    ("M", 3, 1, 0), ("R", 9), ("X", 1), ("Y", 6), ("Y", 7), ("Y", 8), ("Fyw", 1), ("Fyw", 3), ("X", 2), ("Fzm", 3),
+    ("Y", 9), ("Fxc3", 3), ("Fzp", 2), ("M", 1, 1, 0), ("Fyw", 2), ("Fyw", 0), ("M", 3, 0, 1), ("X", 3), ("U", 0),
+    ("X", 4), ("U", 1), ("M", 2, 0, 0), ("Fxc3", 2), ("M", 1, 1, 1), ("T", 0), ("M", 2, 1, 1), ("T", 1),
+    ("M", 2, 0, 1), ("M", 2, 1, 0), ("M", 3, 1, 1), ("S", 0), ("S", 1),
 )
 NT = (((1,), (1,)), ((), ()))
+TN = (((0,), (1,)), ((), ()))
 
 
 class Net:
@@ -75,8 +77,14 @@
             pltpu.make_async_copy(whole, whole, self.send_sems.at[at]).wait()
 
 
-RECV_SEMS = 90
+RECV_SEMS = 88
 SEND_SEMS = 3
+
+
+def update_rows(rows, step_all, basis, weight, out):
+    step = step_all[:, :, :, rows].reshape(RANK, 512)
+    change = lax.dot_general(step, basis[...], TN, preferred_element_type=F32)
+    out[0:512, :] = (weight[rows, :].astype(F32) - learn_rate * change).astype(BF16)
 
 
 def exchange(
@@ -163,6 +171,8 @@
             "z-": (zm, (dz + 1) % 4, h),
             "xc": (xc, dz, 1 - h),
             "xs": (xs, dz, h),
+            "y+": (yp, dz, h),
+            "y-": (ym, dz, h),
         }[way]
         src, dst = ((dz * 2 + h) * 512 + start, (to_dz * 2 + to_h) * 512 + start)
         if not isinstance(start, int):
@@ -277,7 +287,7 @@
         cols = part(2 * OWN_AT + 2 * j)[3]
         net.recv(("step", j))
         ours = step_all.at[:, c, :, cols]
-        net.start(("ss",), ours, ours, sib)
+        net.start(("ss", j), ours, ours, sib)
 
     def D2():
         loads["other_codes"].wait()
@@ -314,17 +324,31 @@
         net.recv(("xs0", i))
         wsend(("zo1", i), "z-", 0, 1, i * 128, 128)
 
+    parity = y % 2
+
     def Fr3(i):
         net.recv(("zo3", i))
-        wsend(("zr3", i), "z+", 3, 1, i * 128, 128)
+        wsend(("zr3", i), "z+", 3, 1, half_of(i, parity), 64)
 
     def Fr1(i):
         net.recv(("zo1", i))
-        wsend(("zr1", i), "z-", 1, 1, i * 128, 128)
+        wsend(("zr1", i), "z-", 1, 1, half_of(i, parity), 64)
 
     def F2(i):
         net.recv(("zpp", i) if i < 2 else ("zmm", i))
-        wsend(("xc2", i), "xc", 2, 0, half_of(i, xlo), 64)
+        wsend(("xc2", i), "xc", 2, 0, half_of(i, parity) + xlo * 32, 32)
+
+    def Fxc2(i):
+        net.recv(("xc2", i))
+        wsend(("xs2", i), "xs", 2, 1, half_of(i, parity) + (1 - xlo) * 32, 32)
+
+    def Fyw(i):
+        if i in (0, 3):
+            net.recv(("zr%d" % (1 if i else 3), i))
+        else:
+            net.recv(("xc2", i))
+            net.recv(("xs2", i))
+        wsend(("yw", i), "y+" if i < 2 else "y-", 2, 1, half_of(i, parity), 64)
 
     def M(dz, h, u):
         for i in (2 * u, 2 * u + 1):
@@ -338,6 +362,8 @@
             else:
                 net.recv(("xc%d" % dz, i))
                 net.recv(("xs%d" % dz, i))
+            if (dz, h) == (2, 1):
+                net.recv(("yw", i))
         net.recv(("og",))
         slot = dz * 2 + h
         fsdp = ((z + dz) % 4) * 2 + (1 - xhi if h else xhi)
@@ -369,12 +395,15 @@
         wsend(("zm", 0), "z-", 0, 0, 0, 128)
 
     steps = dict(
-        W0b=W0b,
+        W0b=W0b, Fyw=Fyw,
         P=P, C=C, E=E, R=R, Y=Y, X=X, U=U, T=T, S=S, M=M, D2=D2, Fzp=Fzp, Fzm=Fzm, Fo3=Fo3, Fo1=Fo1, Fr3=Fr3,
-        Fr1=Fr1, F2=F2, Fxc0=forward_x(0), Fxc1=forward_x(1), Fxc2=forward_x(2), Fxc3=forward_x(3),
+        Fr1=Fr1, F2=F2, Fxc0=forward_x(0), Fxc1=forward_x(1), Fxc2=Fxc2, Fxc3=forward_x(3),
     )
     for name, *place in ORDER:
         steps[name](*place)
+
+    net.recv(("ss", 0))
+    update_rows(slice(0, 512), step_all, bas, weight, weight)
     net.finish()
 
 
@@ -384,16 +413,13 @@
     ]
     copies.append(pltpu.make_async_copy(first_new, first_out, sems.at[4]))
     copies.append(pltpu.make_async_copy(second_new, second_out, sems.at[5]))
+    copies.append(pltpu.make_async_copy(weight.at[pl.ds(0, 512)], weight_out.at[pl.ds(0, 512)], sems.at[6]))
     for copy in copies:
         copy.start()
-    for i in range(4):
-        rows = slice(i * 256, (i + 1) * 256)
-        step = jnp.transpose(step_all[:, :, :, rows].reshape(RANK, 256))
-        change = lax.dot_general(step, basis[...], NT, preferred_element_type=F32)
-        nw[rows, :] = (weight[rows, :].astype(F32) - learn_rate * change).astype(BF16)
-        copy = pltpu.make_async_copy(nw.at[pl.ds(i * 256, 256)], weight_out.at[pl.ds(i * 256, 256)], sems.at[6 + i])
-        copy.start()
-        copies.append(copy)
+    update_rows(slice(512, 1024), step_all, basis, weight, nw)
+    copy = pltpu.make_async_copy(nw, weight_out.at[pl.ds(512, 512)], sems.at[7])
+    copy.start()
+    copies.append(copy)
     for copy in copies:
         copy.wait()
 
@@ -456,7 +482,7 @@
         ),
         in_specs=[vmem_spec] * 6,
         out_specs=(any_spec,) * 4,
-        scratch_shapes=[pltpu.VMEM((1024, 1024), BF16), pltpu.SemaphoreType.DMA((10,))],
+        scratch_shapes=[pltpu.VMEM((512, 1024), BF16), pltpu.SemaphoreType.DMA((8,))],
         compiler_params=pltpu.CompilerParams(vmem_limit_bytes=16 * 2**20),
         cost_estimate=pl.CostEstimate(flops=10**9, bytes_accessed=14 * 2**20, transcendentals=0),
     )(*held, proj_basis)

time: 72.8 us -> 71.3 us (0.979)
  Pallas kernels: 71.9 us -> 70.3 us
    pallas_call x1, Pallas kernels: 67.8 us -> 66.3 us  [shards(): pl.pallas_call(exchange, name='exchange', out_shape=(pltpu.VMEM((TOK, D),...]
where the time goes in v3:
time: 71.3 us; the launch traced here: 71.2 us
  Pallas kernels  70.3 us (99%)
  between operations  0.82 us (1%)
    pallas_call x1, Pallas kernels, shards(): pl.pallas_call(exchange, name='exchange', out_shape=(pltpu.VMEM((TOK, D),...  66.3 us
    pallas_call x1, Pallas kernels, shards(): pl.pallas_call(write_out, name='write_out', out_shape=(jax.ShapeDtypeStru...  4.08 us

profile of v3, /device:TPU:1, one launch (start us, length us, event | category | flops | bytes accessed | tf_op | source)
XLA Modules:
  0.0 71.2 jit_solution(10238708443631218181)
XLA Ops:
  0.6 0.0 copy-start
  0.6 66.3 %exchange.1 = (bf16[512,8192]{1,0:T(8,128)(2,1)S(1)}, bf16[8,2,32,1024]{3,2,1,0:T(8,128)(2,1)S(1)}, f32[32,1024]{1,0:T(8,128)S(1)}, f32[32,1024]{1,0:T(8,128)S(1)}, bf16[1024,1024]{1,0:T(8,128)(2,1)S(1)}) custom-call(bf16[512,8192]{1,0:T(8,128)(2,1)} %tokens.1, bf16[512,1024]{1,0:T(8,128)(2,1)} %out_grad.1, bf16[1024,1024]{1,0:T(8,128)(2,1)} %codes.1, ...), custom_call_target="tpu_custom_call" | custom-call | flops 14000000000 | bytes 13631488 | tf_op jit(solution)/shard_map/exchange/pallas_call | solution.py:430
  66.9 0.0 copy-done
  66.9 4.1 %write_out.1 = (bf16[512,8192]{1,0:T(8,128)(2,1)}, f32[32,1024]{1,0:T(8,128)}, f32[32,1024]{1,0:T(8,128)}, bf16[1024,1024]{1,0:T(8,128)(2,1)}) custom-call(bf16[512,8192]{1,0:T(8,128)(2,1)S(1)} %get-tuple-element.13.ig, bf16[8,2,32,1024]{3,2,1,0:T(8,128)(2,1)S(1)} %get-tuple-element.14.step_all, f32[32,1024]{1,0:T(8,128)S(1)} %get-tuple-element.15.first_new, ...), custom_call_target="tpu_custom_call" | custom-call | flops 1000000000 | bytes 14680064 | tf_op jit(solution)/shard_map/write_out/pallas_call | solution.py:474
Async XLA Ops:
  0.6 66.3 %copy-start = (bf16[1024,512]{1,0:T(8,128)(2,1)S(1)}, bf16[1024,512]{1,0:T(8,128)(2,1)}, u32[]{:S(2)}) copy-start(bf16[1024,512]{1,0:T(8,128)(2,1)} %basis.3) | copy-start | bytes 3145732

commit v4 on v3

--- a/solution.py
+++ b/solution.py
@@ -23,18 +23,18 @@
 CHUNKS = ((1, 0, 1024), (2, 0, 1024), (3, 0, 1024), (0, 0, 512), (0, 512, 512))
 OWN_AT = 3
 ORDER = (
-    ("P", 0), ("W0b",), ("P", 1), ("P", 2), ("C", 0), ("C", 1), ("C", 2), ("E", 0), ("P", 3), ("Fxc0", 0), ("P", 4),
-    ("M", 0, 0, 0), ("Fxc0", 3), ("C", 3), ("P", 5), ("P", 6), ("Fxc0", 1), ("E", 2), ("C", 4), ("M", 0, 0, 1),
-    ("R", 0), ("C", 5), ("Fzm", 2), ("E", 1), ("E", 3), ("P", 7), ("Fxc0", 2), ("Fzp", 1), ("Fxc1", 2), ("R", 1),
-    ("Fzm", 1), ("R", 3), ("P", 8), ("Y", 0), ("M", 3, 0, 0), ("C", 6), ("E", 5), ("M", 0, 1, 0), ("R", 5), ("C", 8),
-    ("P", 9), ("R", 2), ("Fxc3", 1), ("Fzm", 0), ("Fo3", 0), ("Fxc1", 1), ("Fo1", 3), ("M", 1, 0, 1), ("R", 4),
-    ("C", 7), ("Fzp", 3), ("Y", 1), ("R", 6), ("E", 4), ("Y", 3), ("M", 1, 0, 0), ("F2", 1), ("Fzp", 0),
-    ("M", 0, 1, 1), ("Fxc1", 0), ("E", 6), ("F2", 2), ("Y", 5), ("C", 9), ("D2",), ("Y", 2), ("R", 8), ("R", 7),
-    ("Fr3", 0), ("Fxc2", 1), ("Fr1", 3), ("E", 7), ("X", 0), ("E", 9), ("Y", 4), ("E", 8), ("Fxc2", 2),
-    ("M", 3, 1, 0), ("R", 9), ("X", 1), ("Y", 6), ("Y", 7), ("Y", 8), ("Fyw", 1), ("Fyw", 3), ("X", 2), ("Fzm", 3),
-    ("Y", 9), ("Fxc3", 3), ("Fzp", 2), ("M", 1, 1, 0), ("Fyw", 2), ("Fyw", 0), ("M", 3, 0, 1), ("X", 3), ("U", 0),
-    ("X", 4), ("U", 1), ("M", 2, 0, 0), ("Fxc3", 2), ("M", 1, 1, 1), ("T", 0), ("M", 2, 1, 1), ("T", 1),
-    ("M", 2, 0, 1), ("M", 2, 1, 0), ("M", 3, 1, 1), ("S", 0), ("S", 1),
+    ("P", 0), ("W0b",), ("P", 1), ("P", 2), ("C", 1), ("C", 0), ("P", 3), ("P", 4), ("E", 0), ("C", 2), ("Fxc0", 0),
+    ("Fxc0", 3), ("P", 5), ("Fxc0", 1), ("C", 3), ("R", 0), ("C", 4), ("P", 6), ("Fzm", 2), ("P", 7), ("Fxc0", 2),
+    ("C", 5), ("E", 3), ("Fzp", 1), ("R", 2), ("Y", 0), ("C", 7), ("Fo3", 0), ("P", 8), ("R", 3), ("Fo1", 3),
+    ("Fxc1", 2), ("C", 6), ("E", 2), ("R", 4), ("R", 1), ("Fzm", 1), ("E", 4), ("C", 8), ("M", 0, 1, 0), ("Fxc3", 1),
+    ("M", 3, 0, 0), ("R", 7), ("M", 0, 1, 1), ("M", 1, 0, 1), ("Fzm", 0), ("R", 5), ("Y", 3), ("M", 1, 0, 0),
+    ("P", 9), ("Y", 2), ("E", 1), ("Fxc1", 1), ("E", 5), ("D2",), ("Fxc1", 0), ("E", 7), ("R", 6), ("R", 8), ("C", 9),
+    ("F2", 1), ("M", 3, 0, 1), ("Y", 4), ("E", 6), ("X", 1), ("Y", 1), ("F2", 2), ("Fr1", 3), ("E", 9), ("Fzp", 3),
+    ("E", 8), ("Fxc2", 1), ("Fr3", 0), ("M", 1, 1, 0), ("Y", 5), ("Fxc2", 2), ("X", 0), ("R", 9), ("Y", 6),
+    ("Fyw", 1), ("Y", 8), ("Fzp", 2), ("Y", 7), ("Fyw", 3), ("Fzp", 0), ("X", 2), ("M", 3, 1, 0), ("Fzm", 3),
+    ("Fyw", 0), ("Y", 9), ("Fyw", 2), ("Fxc3", 3), ("M", 0, 0, 0), ("X", 3), ("U", 0), ("X", 4), ("M", 1, 1, 1),
+    ("U", 1), ("Fxc3", 2), ("M", 0, 0, 1), ("T", 0), ("M", 2, 1, 1), ("T", 1), ("M", 2, 0, 0), ("M", 2, 1, 0),
+    ("M", 2, 0, 1), ("S", 0), ("M", 3, 1, 1), ("S", 1),
 )
 NT = (((1,), (1,)), ((), ()))
 TN = (((0,), (1,)), ((), ()))
@@ -77,7 +77,7 @@
             pltpu.make_async_copy(whole, whole, self.send_sems.at[at]).wait()
 
 
-RECV_SEMS = 88
+RECV_SEMS = 86
 SEND_SEMS = 3
 
 
@@ -119,8 +119,14 @@
 
     half = pl.multiple_of(c * 512, 512)
     other = pl.multiple_of(512 - c * 512, 512)
+
+    def load_codes(name, first, size):
+        rows = pl.ds(pl.multiple_of(half + first, 128), size)
+        load(name, codes.at[rows], cod.at[rows])
+
     load("scales", scales, sca)
-    load("own_codes", codes.at[pl.ds(half, 512)], cod.at[pl.ds(half, 512)])
+    load_codes("codes_0", 0, 128)
+    load_codes("codes_3", 384, 128)
     load("og", out_grad, og.at[0])
     load("basis", basis, bas)
 
@@ -135,11 +141,8 @@
         src = tokens.at[:, pl.ds(pl.multiple_of(at, 512), width)]
         load(("tok", q), src, tok.at[q % 4, :, :width])
 
-    for q in range(4):
-        load_tokens(q)
-    load("other_codes", codes.at[pl.ds(other, 512)], cod.at[pl.ds(other, 512)])
-    load("fp", first_prev, fp)
-    load("sp", second_prev, sp)
+    load_tokens(0)
+    load_codes("codes_12", 128, 256)
 
     barrier = pltpu.get_barrier_semaphore()
     for peer in peers:
@@ -157,7 +160,8 @@
                     W[i * 128 : (i + 1) * 128, cols] = w
 
     loads["scales"].wait()
-    loads["own_codes"].wait()
+    loads["codes_0"].wait()
+    loads["codes_3"].wait()
     dequantize(half, (0, 3), True)
     pl.semaphore_wait(barrier, len(peers))
     net = Net(send_sems, recv_sems, W)
@@ -183,6 +187,7 @@
     wsend(("zm", 3), "z-", 0, 0, 384, 128)
     wsend(("xc0", 0), "xc", 0, 0, half_of(0, xlo), 64)
     wsend(("xc0", 3), "xc", 0, 0, half_of(3, xlo), 64)
+    load_tokens(1)
 
     loads["og"].wait()
     loads["basis"].wait()
@@ -201,7 +206,7 @@
             acc = jnp.dot(proj_t[...], tok[q % 4, :, i : i + 256], preferred_element_type=F32)
             own[q % OWN, :, i : i + 256] = acc[:256]
             sib_out[slot, :, span.start + i : span.start + i + 256] = acc[256:].astype(BF16)
-        if q + 4 < 2 * len(CHUNKS):
+        if 0 < q < 2 * len(CHUNKS) - 4:
             load_tokens(q + 4)
 
     def P(q):
@@ -209,6 +214,11 @@
         multiply(q)
         if q == 0:
             net.start(("og",), og.at[0], og.at[1], sib)
+            for later in (2, 3, 4):
+                load_tokens(later)
+            load("other_codes", codes.at[pl.ds(other, 512)], cod.at[pl.ds(other, 512)])
+            load("fp", first_prev, fp)
+            load("sp", second_prev, sp)
         net.start(("sib", q), sib_out.at[slot, :, cols], sib_in.at[slot, :, cols], sib)
 
     def C(q):
@@ -348,7 +358,7 @@
         else:
             net.recv(("xc2", i))
             net.recv(("xs2", i))
-        wsend(("yw", i), "y+" if i < 2 else "y-", 2, 1, half_of(i, parity), 64)
+        wsend(("yw", i // 2), "y+" if i < 2 else "y-", 2, 1, half_of(i, parity), 64)
 
     def M(dz, h, u):
         for i in (2 * u, 2 * u + 1):
@@ -363,7 +373,7 @@
                 net.recv(("xc%d" % dz, i))
                 net.recv(("xs%d" % dz, i))
             if (dz, h) == (2, 1):
-                net.recv(("yw", i))
+                net.recv(("yw", u))
         net.recv(("og",))
         slot = dz * 2 + h
         fsdp = ((z + dz) % 4) * 2 + (1 - xhi if h else xhi)
@@ -384,6 +394,7 @@
         net.start(("ig",), stage.at[slot, u], ig.at[:, cols], sib)
 
     def W0b():
+        loads["codes_12"].wait()
         dequantize(half, (1, 2), True)
         wsend(("zp", 1), "z+", 0, 0, 128, 128)
         wsend(("zm", 2), "z-", 0, 0, 256, 128)
@@ -464,7 +475,7 @@
             pltpu.VMEM((32, 1024), F32),
             pltpu.SemaphoreType.DMA((SEND_SEMS,)),
             pltpu.SemaphoreType.DMA((RECV_SEMS,)),
-            pltpu.SemaphoreType.DMA((17,)),
+            pltpu.SemaphoreType.DMA((19,)),
         ],
         compiler_params=pltpu.CompilerParams(
             collective_id=0, has_side_effects=True, vmem_limit_bytes=50 * 2**20

time: 71.3 us -> 70.7 us (level)
  no operation moved by 1% of the time
where the time goes in v4:
time: 70.7 us; the launch traced here: 70.6 us
  Pallas kernels  69.8 us (99%)
  between operations  0.82 us (1%)
    pallas_call x1, Pallas kernels, shards(): pl.pallas_call(exchange, name='exchange', out_shape=(pltpu.VMEM((TOK, D),...  65.7 us
    pallas_call x1, Pallas kernels, shards(): pl.pallas_call(write_out, name='write_out', out_shape=(jax.ShapeDtypeStru...  4.08 us

profile of v4, /device:TPU:1, one launch (start us, length us, event | category | flops | bytes accessed | tf_op | source)
XLA Modules:
  0.0 70.6 jit_solution(14699496389171819575)
XLA Ops:
  0.6 0.0 copy-start
  0.6 65.7 %exchange.1 = (bf16[512,8192]{1,0:T(8,128)(2,1)S(1)}, bf16[8,2,32,1024]{3,2,1,0:T(8,128)(2,1)S(1)}, f32[32,1024]{1,0:T(8,128)S(1)}, f32[32,1024]{1,0:T(8,128)S(1)}, bf16[1024,1024]{1,0:T(8,128)(2,1)S(1)}) custom-call(bf16[512,8192]{1,0:T(8,128)(2,1)} %tokens.1, bf16[512,1024]{1,0:T(8,128)(2,1)} %out_grad.1, bf16[1024,1024]{1,0:T(8,128)(2,1)} %codes.1, ...), custom_call_target="tpu_custom_call" | custom-call | flops 14000000000 | bytes 13631488 | tf_op jit(solution)/shard_map/exchange/pallas_call | solution.py:441
  66.4 0.0 copy-done
  66.4 4.1 %write_out.1 = (bf16[512,8192]{1,0:T(8,128)(2,1)}, f32[32,1024]{1,0:T(8,128)}, f32[32,1024]{1,0:T(8,128)}, bf16[1024,1024]{1,0:T(8,128)(2,1)}) custom-call(bf16[512,8192]{1,0:T(8,128)(2,1)S(1)} %get-tuple-element.13.ig, bf16[8,2,32,1024]{3,2,1,0:T(8,128)(2,1)S(1)} %get-tuple-element.14.step_all, f32[32,1024]{1,0:T(8,128)S(1)} %get-tuple-element.15.first_new, ...), custom_call_target="tpu_custom_call" | custom-call | flops 1000000000 | bytes 14680064 | tf_op jit(solution)/shard_map/write_out/pallas_call | solution.py:485
Async XLA Ops:
  0.6 65.7 %copy-start = (bf16[1024,512]{1,0:T(8,128)(2,1)S(1)}, bf16[1024,512]{1,0:T(8,128)(2,1)}, u32[]{:S(2)}) copy-start(bf16[1024,512]{1,0:T(8,128)(2,1)} %basis.3) | copy-start | bytes 3145732
